TPU v7x, 32 devices: a whole 2x2x4 slice. The times are simulated.
32 devices in a mesh: outer: 4 (over z), inner: 8 (over y, x, core).
Axes of the slice: x: 2, y: 2, z: 4, core: 2. Of those that a mesh axis runs over, the one named last changes fastest.
Arguments:
- context: bfloat16 [4096, 4096], P(('outer', 'inner')), may hold values from -5 to 5
- query_acts: bfloat16 [64, 4096], replicated, may hold values from -5 to 5
- norm_gain: float32 [4096], replicated, may hold values from 0.25 to 1.75
- w_query: bfloat16 [4096, 2048], P('inner'), may hold values from -0.078125 to 0.078125
- w_key: bfloat16 [4096, 512], P('inner'), may hold values from -0.453125 to 0.453125
- value_weight: bfloat16 [4096, 512], P('inner'), may hold values from -0.09375 to 0.09375
- lengths: int32 [32], replicated, may hold values from 64 to 128, as said below
Outputs:
- block_out: bfloat16 [4096, 2048], P(('outer', 'inner'))
- query_out: bfloat16 [64, 2048], replicated
Inputs may be any that keep to these rules, and one draw needn't show every extreme that they name: `lengths`: valid tokens of a block are its first ones; the rest of it is padding.
All inputs are finite; a program needn't handle non-finite values.
Results may differ from a plain program's by a relative error of at most 0.004.
The roundings to bfloat16 on the way count: a program that leaves them out, or rounds other values in their place, can miss the bound.
Values may be sent and summed in bfloat16 or wider, within the bound.
A program may use at most 320 MiB of HBM per device.

v0:
```python
import jax
import jax.numpy as jnp
from jax import lax
from jax.experimental import pallas as pl
from jax.experimental.pallas import tpu as pltpu
from jax.sharding import PartitionSpec as P

QUERY_HEADS = 16
KEY_VALUE_HEADS = 4
HEAD_SIZE = 128


epsilon = 1e-05


def broadcast(block, axis, owner):
    block = jnp.where(lax.axis_index(axis) == owner, block, jnp.zeros_like(block))
    return lax.psum(block, axis)


def normalize(matrix, norm_gain):
    widened = matrix.astype(jnp.float32)
    factor = lax.rsqrt(jnp.mean(widened * widened, axis=-1, keepdims=True) + epsilon)
    return (widened * factor * norm_gain).astype(jnp.bfloat16)


def chip_peer(chip, step):
    offset = (step + 1) % 4
    return (chip // 2 + offset // 2) % 2 * 2 + (chip + offset) % 2


def normalize_rows(source, gain, first, count):
    widened = source[pl.ds(first, count), :].astype(jnp.float32)
    factor = lax.rsqrt(jnp.mean(widened * widened, axis=-1, keepdims=True) + epsilon)
    return (widened * factor * gain[...]).astype(jnp.bfloat16)


def masked_softmax(rows, keys, values, allowed):
    scores = lax.dot_general(
        rows, keys, (((1,), (1,)), ((), ())), preferred_element_type=jnp.float32
    ) * HEAD_SIZE ** (-0.5)
    scores = jnp.where(allowed, scores, -jnp.inf)
    peak = jnp.max(scores, axis=-1, keepdims=True)
    weights = jnp.exp(scores - peak)
    sum_exp = jnp.sum(weights, axis=-1, keepdims=True)
    numerator = jnp.dot(
        weights.astype(jnp.bfloat16), values, preferred_element_type=jnp.float32
    )
    return peak, sum_exp, numerator


def iota(shape, dim):
    return lax.broadcasted_iota(jnp.int32, shape, dim)


def head_rows(source, head_group):
    first = 1024 + head_group * 512
    return jnp.concatenate(
        [source[:, first + g * 128 : first + (g + 1) * 128] for g in range(4)], axis=0
    )


def store_partials(target, head_group, partials):
    peak, sum_exp, numerator = partials
    row, lane = iota((32, 128), 0), iota((32, 128), 1)
    for b in range(8):
        part = slice(b * 32, (b + 1) * 32)
        target[head_group * 8 + b, 0:32] = numerator[part]
        stats = jnp.where(lane == row, peak[part], 0.0) + jnp.where(
            lane == row + 32, sum_exp[part], 0.0
        )
        target[head_group * 8 + b, 32:40] = jnp.broadcast_to(
            jnp.sum(stats, axis=0, keepdims=True), (8, 128)
        )


def stat_column(stats, shift):
    row, lane = iota((32, 128), 0), iota((32, 128), 1)
    spread_stats = jnp.broadcast_to(stats, (32, 128))
    return jnp.sum(
        jnp.where(lane == row + shift, spread_stats, 0.0), axis=1, keepdims=True
    )


def layer_kernel(
    context_rows, query_acts, gain, w_query, w_key, value_weight, lengths, block_out, query_out,
    twin_query, twin_key, twin_value, sliced, query_sliced, gathered, partial, first_sum, passed,
    second_sum, query_sums, query_arrived, query_mine, query_parts, context, query,
    anchor, partials, own_partials, received, merged, merged_all,
    twin_send, twin_recv, row_send, row_recv, first_send, first_recv, passed_send, passed_recv,
    second_send, second_recv, query_send, query_recv, spread_send, spread_recv,
    scatter_send, column_send, plane_send, anchor_recv,
    partial_send, partial_recv, merged_send, merged_recv,
):
    outer, inner = lax.axis_index("outer"), lax.axis_index("inner")
    outers, inners = lax.axis_size("outer"), lax.axis_size("inner")
    devices = outers * inners
    me = outer * inners + inner
    chip, core = inner // 2, inner % 2
    twin = chip * 2 + 1 - core

    def peer(step):
        return chip_peer(chip, step)

    def remote(source, target, send, recv, to_outer, to_inner):
        return pltpu.make_async_remote_copy(
            src_ref=source, dst_ref=target, send_sem=send, recv_sem=recv,
            device_id={"outer": to_outer, "inner": to_inner},
            device_id_type=pl.DeviceIdType.MESH,
        )

    barrier = pltpu.get_barrier_semaphore()

    def greet(t, carry):
        other = (me + t) % devices
        pl.semaphore_signal(
            barrier, inc=1, device_id={"outer": other // inners, "inner": other % inners},
            device_id_type=pl.DeviceIdType.MESH,
        )
        return carry

    lax.fori_loop(1, devices, greet, 0)
    pl.semaphore_wait(barrier, devices - 1)

    weight_copies = [
        remote(mine, theirs, twin_send.at[k], twin_recv.at[k], outer, twin)
        for k, (mine, theirs) in enumerate(
            ((w_key, twin_key), (value_weight, twin_value), (w_query, twin_query))
        )
    ]
    for copy in weight_copies:
        copy.start()

    @pl.loop(0, context_rows.shape[0] // 16)
    def _(index):
        first = pl.multiple_of(index * 16, 16)
        rows = normalize_rows(context_rows, gain, first, 16)
        for k in range(4):
            sliced[k, pl.ds(first, 16), :] = rows[:, k * 1024 : (k + 1) * 1024]

    row_copies = [
        remote(
            sliced.at[peer(step)], gathered.at[step], row_send.at[step], row_recv.at[step],
            outer, peer(step) * 2 + core,
        )
        for step in range(3)
    ]
    for step in (2, 0, 1):
        row_copies[step].start()

    @pl.loop(0, query_acts.shape[0] // 16)
    def _(index):
        first = pl.multiple_of(index * 16, 16)
        rows = normalize_rows(query_acts, gain, first, 16)
        for k in range(4):
            query_sliced[k, pl.ds(first, 16), :] = rows[:, k * 1024 : (k + 1) * 1024]

    gathered[3] = sliced[chip]
    for copy in weight_copies:
        copy.wait()

    def tiles(k):
        if k < 2:
            return (w_key, value_weight)[k][...], (twin_key, twin_value)[k][...]
        columns = slice((k - 2) * 512, (k - 1) * 512)
        return w_query[:, columns], twin_query[:, columns]

    own_columns = pl.ds(pl.multiple_of(core * 512, 512), 512)
    twin_columns = pl.ds(pl.multiple_of((1 - core) * 512, 512), 512)

    def product(source, index, k):
        own_tile, twin_tile = tiles(k)
        return jnp.dot(
            source[index, :, own_columns], own_tile, preferred_element_type=jnp.float32
        ) + jnp.dot(
            source[index, :, twin_columns], twin_tile, preferred_element_type=jnp.float32
        )

    for k in range(6):
        query_sums[:, k * 512 : (k + 1) * 512] = product(query_sliced, chip, k)

    def query_part(other):
        return pl.ds(pl.multiple_of(other * 16 + core * 8, 8), 8)

    query_copies = [
        remote(
            query_sums.at[query_part(peer(step))], query_arrived.at[step], query_send.at[step],
            query_recv.at[step], outer, peer(step) * 2 + core,
        )
        for step in range(3)
    ]
    for copy in query_copies:
        copy.start()

    def first_copy(k):
        return remote(
            partial.at[k % 2, k], first_sum.at[k], first_send.at[k], first_recv.at[k],
            outer, peer(k % 2) * 2 + core,
        )

    def passed_copy(k):
        return remote(
            partial.at[2, k], passed.at[k], passed_send.at[k], passed_recv.at[k],
            outer, peer(k % 2) * 2 + core,
        )

    def second_copy(k):
        return remote(
            partial.at[1 - k % 2, k], second_sum.at[k], second_send.at[k], second_recv.at[k],
            outer, peer(1 - k % 2) * 2 + core,
        )

    def multiply(k):
        def one(step, carry):
            partial[step, k] = product(gathered, step, k)
            return carry

        lax.fori_loop(0, 4, one, 0)
        passed_copy(k).start()
        first_copy(k).start()

    def relay(k):
        passed_copy(k).wait()
        partial[1 - k % 2, k] = partial[1 - k % 2, k] + passed[k]
        second_copy(k).start()

    def settle(k):
        first_copy(k).wait()
        second_copy(k).wait()
        total = partial[3, k] + first_sum[k] + second_sum[k]
        context[:, k * 512 : (k + 1) * 512] = total.astype(jnp.bfloat16)

    for step in range(3):
        row_copies[step].wait()
    for k in range(4):
        multiply(k)

    for copy in query_copies:
        copy.wait()
    query_mine[...] = (
        query_sums[query_part(chip), :] + query_arrived[0] + query_arrived[1] + query_arrived[2]
    ).astype(jnp.bfloat16).astype(jnp.float32)

    def spread_copy(other, slot):
        return remote(
            query_mine, query_parts.at[slot], spread_send.at[other], spread_recv.at[slot],
            outer, other,
        )

    def send_query(t, carry):
        spread_copy((inner + t) % inners, inner).start()
        return carry

    lax.fori_loop(1, inners, send_query, 0)
    query_parts[inner] = query_mine[...]
    relay(0)
    relay(1)
    for k in range(4, 6):
        multiply(k)

    def wait_query(t, carry):
        other = (inner + t) % inners
        spread_copy(other, other).wait()
        return carry

    lax.fori_loop(1, inners, wait_query, 0)
    for pair in range(4):
        query[pair * 16 : (pair + 1) * 16] = jnp.concatenate(
            [query_parts[pair * 2], query_parts[pair * 2 + 1]], axis=0
        ).astype(jnp.bfloat16)
    settle(0)
    settle(1)

    def scatter_copy(j):
        return remote(
            context.at[:, pl.ds(j * 128, 128)], anchor.at[j], scatter_send.at[j],
            anchor_recv.at[j], 0, j,
        )

    @pl.when(me == 0)
    def _():
        for j in range(1, 8):
            scatter_copy(j).start()
        anchor[0] = context[:, 0:128]

    own_length, anchor_length = lengths[me], lengths[0]

    for h in range(4):
        keys = context[:, h * 128 : (h + 1) * 128]
        values = context[:, 512 + h * 128 : 512 + (h + 1) * 128]
        reached = iota((256, 128), 1) < own_length
        store_partials(partials, h, masked_softmax(head_rows(query, h), keys, values, reached))

    def partial_copy(other):
        return lambda slot: remote(
            partials.at[other], received.at[slot], partial_send.at[other], partial_recv.at[slot],
            other // inners, other % inners,
        )

    def send_partial(t, carry):
        partial_copy((me + t) % devices)(me).start()
        return carry

    lax.fori_loop(1, devices, send_partial, 0)

    relay(2)
    relay(3)

    def column_copy(o):
        return remote(
            anchor.at[inner], anchor.at[inner], column_send.at[o], anchor_recv.at[inner], o, inner
        )

    def plane_copy(j, slot):
        return remote(
            anchor.at[slot], anchor.at[slot], plane_send.at[j], anchor_recv.at[slot], outer, j
        )

    @pl.when(me != 0)
    def _():
        plane_copy(inner, inner).wait_recv()

    @pl.when(outer == 0)
    def _():
        for o in range(1, 4):
            column_copy(o).start()

    def send_plane(t, carry):
        plane_copy((inner + t) % inners, inner).start()
        return carry

    lax.fori_loop(1, inners, send_plane, 0)

    for h in range(4):
        keys = query[:, h * 128 : (h + 1) * 128]
        values = query[:, 512 + h * 128 : 512 + (h + 1) * 128]
        causal = iota((256, 64), 0) % 64 >= iota((256, 64), 1)
        store_partials(own_partials, h, masked_softmax(head_rows(query, h), keys, values, causal))
    received[me] = partials[me]
    received[devices] = own_partials[me]

    relay(4)
    relay(5)

    def wait_partial(t, carry):
        other = (me + t) % devices
        partial_copy(other)(other).wait()
        return carry

    lax.fori_loop(1, devices, wait_partial, 0)

    def highest(s, peak):
        return jnp.maximum(peak, stat_column(received[s, 32:33], 0))

    top = lax.fori_loop(
        0, devices + 1, highest, jnp.full((32, 1), -jnp.inf, jnp.float32)
    )

    def add_up(s, carry):
        total, numerator = carry
        factor = jnp.exp(stat_column(received[s, 32:33], 0) - top)
        return (
            total + stat_column(received[s, 32:33], 32) * factor,
            numerator + received[s, 0:32] * factor,
        )

    total, numerator = lax.fori_loop(
        0, devices + 1, add_up,
        (jnp.zeros((32, 1), jnp.float32), jnp.zeros((32, 128), jnp.float32)),
    )
    merged[...] = (numerator / total).astype(jnp.bfloat16)

    def merged_copy(other, slot):
        return remote(
            merged, merged_all.at[slot], merged_send.at[other], merged_recv.at[slot],
            other // inners, other % inners,
        )

    def send_merged(t, carry):
        merged_copy((me + t) % devices, me).start()
        return carry

    lax.fori_loop(1, devices, send_merged, 0)
    merged_all[me] = merged[...]

    for k in range(2, 6):
        settle(k)

    def wait_plane(t, carry):
        other = (inner + t) % inners
        plane_copy(other, inner).wait_send()
        plane_copy(other, other).wait_recv()
        return carry

    lax.fori_loop(1, inners, wait_plane, 0)

    row, column = iota((512, 256), 0) % 128, iota((512, 256), 1)
    place = column % 128
    limit = jnp.where(column < 128, jnp.where(me > 0, anchor_length, 0), own_length)
    allowed = (place < limit) & ((column < 128) | (row >= place))
    for h in range(4):
        keys = jnp.concatenate([anchor[h], context[:, h * 128 : (h + 1) * 128]], axis=0)
        values = jnp.concatenate(
            [anchor[4 + h], context[:, 512 + h * 128 : 512 + (h + 1) * 128]], axis=0
        )
        _, sum_exp, numerator = masked_softmax(head_rows(context, h), keys, values, allowed)
        result = (numerator / sum_exp).astype(jnp.bfloat16)
        for g in range(4):
            block_out[:, (h * 4 + g) * 128 : (h * 4 + g + 1) * 128] = result[
                g * 128 : (g + 1) * 128
            ]

    @pl.when(me == 0)
    def _():
        for j in range(1, 8):
            scatter_copy(j).wait_send()

    @pl.when(outer == 0)
    def _():
        for o in range(1, 4):
            column_copy(o).wait_send()

    def wait_merged(t, carry):
        other = (me + t) % devices
        merged_copy(other, other).wait()
        return carry

    lax.fori_loop(1, devices, wait_merged, 0)
    for d in range(32):
        query_out[d % 2 * 32 : d % 2 * 32 + 32, d // 2 * 128 : d // 2 * 128 + 128] = merged_all[d]


def layer(context, query_acts, norm_gain, w_query, w_key, value_weight, lengths):
    vmem = pl.BlockSpec(memory_space=pltpu.VMEM)
    bf16, f32, dma = jnp.bfloat16, jnp.float32, pltpu.SemaphoreType.DMA
    buffers = [
        ((512, 2048), bf16), ((512, 512), bf16), ((512, 512), bf16),
        ((4, 128, 1024), bf16), ((4, 64, 1024), bf16), ((4, 128, 1024), bf16),
        ((4, 6, 128, 512), f32), ((6, 128, 512), f32), ((6, 128, 512), f32),
        ((6, 128, 512), f32), ((64, 3072), f32), ((3, 8, 3072), f32), ((8, 3072), f32),
        ((8, 8, 3072), f32), ((128, 3072), bf16), ((64, 3072), bf16),
        ((8, 128, 128), bf16), ((32, 40, 128), f32), ((32, 40, 128), f32),
        ((33, 40, 128), f32), ((32, 128), bf16), ((32, 32, 128), bf16),
    ]
    counts = [3, 3, 3, 3, 6, 6, 6, 6, 6, 6, 3, 3, 8, 8, 8, 4, 8, 8, 32, 32, 32, 32]
    return pl.pallas_call(
        layer_kernel,
        out_shape=[
            jax.ShapeDtypeStruct((128, 2048), bf16),
            jax.ShapeDtypeStruct((64, 2048), bf16),
        ],
        in_specs=[vmem] * 6 + [pl.BlockSpec(memory_space=pltpu.SMEM)],
        out_specs=[vmem] * 2,
        scratch_shapes=[pltpu.VMEM(shape, kind) for shape, kind in buffers]
        + [dma((count,)) for count in counts],
        compiler_params=pltpu.CompilerParams(
            collective_id=0, has_side_effects=True, vmem_limit_bytes=56 * 2**20
        ),
        cost_estimate=pl.CostEstimate(
            flops=5 * 10**9, bytes_accessed=8 * 2**20, transcendentals=10**6
        ),
    )(context, query_acts, norm_gain.reshape(1, -1), w_query, w_key, value_weight, lengths)


def attend_part(query_rows, key_row_block, value_matrix, allowed):
    count_of_rows = query_rows.shape[0]
    head_groups = query_rows.reshape(
        count_of_rows, KEY_VALUE_HEADS, QUERY_HEADS // KEY_VALUE_HEADS, HEAD_SIZE
    )
    per_head_keys = key_row_block.reshape(key_row_block.shape[0], KEY_VALUE_HEADS, HEAD_SIZE)
    per_head_values = value_matrix.reshape(value_matrix.shape[0], KEY_VALUE_HEADS, HEAD_SIZE)
    scores = jnp.einsum(
        "rhgd,khd->hgrk", head_groups, per_head_keys, preferred_element_type=jnp.float32
    ) * HEAD_SIZE ** (-0.5)
    scores = jnp.where(allowed, scores, -jnp.inf)
    maxima = jnp.max(scores, axis=-1)
    weights = jnp.exp(scores - maxima[..., None])
    sum_exp = jnp.sum(weights, axis=-1)
    numerator = jnp.einsum(
        "hgrk,khd->rhgd",
        weights.astype(jnp.bfloat16),
        per_head_values,
        preferred_element_type=jnp.float32,
    )
    return (
        maxima.reshape(QUERY_HEADS, count_of_rows),
        sum_exp.reshape(QUERY_HEADS, count_of_rows),
        numerator.reshape(count_of_rows, QUERY_HEADS * HEAD_SIZE),
    )


def spread(factor):
    return jnp.repeat(factor.T, HEAD_SIZE, axis=1)


def combine(former, latter):
    maxima = jnp.maximum(former[0], latter[0])
    scale_one = jnp.exp(former[0] - maxima)
    scale_two = jnp.exp(latter[0] - maxima)
    return (
        maxima,
        former[1] * scale_one + latter[1] * scale_two,
        former[2] * spread(scale_one) + latter[2] * spread(scale_two),
    )


def finish(pieces):
    return (pieces[2] / spread(pieces[1])).astype(jnp.bfloat16)


def share_anchor(stacked):
    return broadcast(stacked, ("outer", "inner"), 0)


def project_all(context, query_acts, norm_gain, w_query, w_key, value_weight):
    normed = jnp.concatenate(
        [normalize(context, norm_gain), normalize(query_acts, norm_gain)], axis=0
    )
    return tuple(
        jnp.dot(
            normed,
            lax.all_gather(weight, "inner", axis=0, tiled=True),
            preferred_element_type=jnp.float32,
        ).astype(jnp.bfloat16)
        for weight in (w_query, w_key, value_weight)
    )


def per_device(context, query_acts, norm_gain, w_query, w_key, value_weight, lengths):
    if (lax.axis_size("outer"), lax.axis_size("inner")) == (4, 8):
        return tuple(
            layer(context, query_acts, norm_gain, w_query, w_key, value_weight, lengths)
        )
    block_rows = context.shape[0]
    projected_q, projected_k, projected_v = project_all(
        context, query_acts, norm_gain, w_query, w_key, value_weight
    )
    anchor = share_anchor(jnp.stack([projected_k[:block_rows], projected_v[:block_rows]]))
    position = lax.axis_index(("outer", "inner"))
    own_length = lengths[position]
    anchor_length = lengths[0]
    places = jnp.arange(block_rows, dtype=jnp.int32)
    causal = places[:, None] >= places[None, :]
    block_q = projected_q[:block_rows]
    block_k = projected_k[:block_rows]
    block_v = projected_v[:block_rows]
    query_q = projected_q[block_rows:]
    query_k = projected_k[block_rows:]
    query_v = projected_v[block_rows:]
    query_count = query_q.shape[0]
    own_allowed = causal & (places[None, :] < own_length)
    anchor_allowed = jnp.broadcast_to(
        (places[None, :] < anchor_length) & (position > 0), (block_rows, block_rows)
    )
    allowed = jnp.concatenate([anchor_allowed, own_allowed], axis=1)
    key_row_block = jnp.concatenate([anchor[0], block_k], axis=0)
    value_rows = jnp.concatenate([anchor[1], block_v], axis=0)
    block_out = finish(attend_part(block_q, key_row_block, value_rows, allowed))
    reached = jnp.broadcast_to(places[None, :] < own_length, (query_count, block_rows))
    block_part = attend_part(query_q, block_k, block_v, reached)
    highest = lax.pmax(block_part[0], ("outer", "inner"))
    rescale = jnp.exp(block_part[0] - highest)
    summed_parts = lax.psum(
        (block_part[1] * rescale, block_part[2] * spread(rescale)), ("outer", "inner")
    )
    merged = (highest, summed_parts[0], summed_parts[1])
    query_places = jnp.arange(query_count, dtype=jnp.int32)
    self_part = attend_part(
        query_q, query_k, query_v, query_places[:, None] >= query_places[None, :]
    )
    return (block_out, finish(combine(merged, self_part)))


def solution(mesh):
    in_specs = (
        P(("outer", "inner"), None),
        P(),
        P(),
        P("inner", None),
        P("inner", None),
        P("inner", None),
        P(),
    )
    out_specs = (P(("outer", "inner"), None), P())
    return jax.shard_map(
        per_device, mesh=mesh, in_specs=in_specs, out_specs=out_specs, check_vma=False
    )
```

profile of v0, /device:TPU:9, one launch (start us, length us, event | category | flops | bytes accessed | tf_op | source)
XLA Modules:
  0.0 108.5 jit_solution(253378835082495500)
XLA Ops:
  0.6 104.3 %shard_map.86 = (bf16[128,2048]{1,0:T(8,128)(2,1)}, bf16[64,2048]{1,0:T(8,128)(2,1)}) custom-call(bf16[128,4096]{1,0:T(8,128)(2,1)} %context_rows.1, bf16[64,4096]{1,0:T(8,128)(2,1)} %query_acts.1, f32[1,4096]{1,0:T(1,128)} %bitcast.1, bf16[512,2048]{1,0:T(8,128)(2,1)} %w_query.1, bf16[512,512]{1,0:T(8,128)(2,1)} %w_key.1, bf16[512,512]{1,0:T(8,128)(2,1)} %value_weight.1, ...), custom_call_target="tpu_custom_call" | custom-call | flops 5000000000 | bytes 8388608 | tf_op jit(solution)/shard_map/pallas_call | solution.py:446
  104.9 1.9 %copy.11 = bf16[128,2048]{1,0:T(8,128)(2,1)} copy(bf16[128,2048]{1,0:T(8,128)(2,1)} %get-tuple-element.4) | data formatting | bytes 1048576
  106.8 1.7 %copy.12 = bf16[64,2048]{1,0:T(8,128)(2,1)} copy(bf16[64,2048]{1,0:T(8,128)(2,1)} %get-tuple-element.5) | data formatting | bytes 524288
where the time goes:
time: 109 us; the launch traced here: 108 us
  Pallas kernels  104 us (95%)
  local copies, waits for them, and re-layouts  3.55 us (3%)
    pallas_call x1, Pallas kernels, layer(): pl.pallas_call(layer_kernel, out_shape=[jax.ShapeDtypeStruct((128, 2048),...  104 us
    unnamed x2, local copies, waits for them, and re-layouts  3.55 us

commit v1 on v0

--- a/solution.py
+++ b/solution.py
@@ -120,17 +120,6 @@
         return carry
 
     lax.fori_loop(1, devices, greet, 0)
-    pl.semaphore_wait(barrier, devices - 1)
-
-    weight_copies = [
-        remote(mine, theirs, twin_send.at[k], twin_recv.at[k], outer, twin)
-        for k, (mine, theirs) in enumerate(
-            ((w_key, twin_key), (value_weight, twin_value), (w_query, twin_query))
-        )
-    ]
-    for copy in weight_copies:
-        copy.start()
-
     @pl.loop(0, context_rows.shape[0] // 16)
     def _(index):
         first = pl.multiple_of(index * 16, 16)
@@ -138,6 +127,8 @@
         for k in range(4):
             sliced[k, pl.ds(first, 16), :] = rows[:, k * 1024 : (k + 1) * 1024]
 
+    pl.semaphore_wait(barrier, devices - 1)
+
     row_copies = [
         remote(
             sliced.at[peer(step)], gathered.at[step], row_send.at[step], row_recv.at[step],
@@ -147,6 +138,15 @@
     ]
     for step in (2, 0, 1):
         row_copies[step].start()
+
+    weight_copies = [
+        remote(mine, theirs, twin_send.at[k], twin_recv.at[k], outer, twin)
+        for k, (mine, theirs) in enumerate(
+            ((w_key, twin_key), (value_weight, twin_value), (w_query, twin_query))
+        )
+    ]
+    for copy in weight_copies:
+        copy.start()
 
     @pl.loop(0, query_acts.shape[0] // 16)
     def _(index):
@@ -241,32 +241,34 @@
         query_sums[query_part(chip), :] + query_arrived[0] + query_arrived[1] + query_arrived[2]
     ).astype(jnp.bfloat16).astype(jnp.float32)
 
-    def spread_copy(other, slot):
-        return remote(
-            query_mine, query_parts.at[slot], spread_send.at[other], spread_recv.at[slot],
-            outer, other,
-        )
-
-    def send_query(t, carry):
-        spread_copy((inner + t) % inners, inner).start()
-        return carry
-
-    lax.fori_loop(1, inners, send_query, 0)
-    query_parts[inner] = query_mine[...]
+    spread_copies = [
+        remote(
+            query_mine, query_parts.at[core, chip], spread_send.at[step], spread_recv.at[step],
+            outer, peer(step) * 2 + core,
+        )
+        for step in range(3)
+    ]
+    for copy in spread_copies:
+        copy.start()
+    query_parts[core, chip] = query_mine[...]
     relay(0)
     relay(1)
     for k in range(4, 6):
         multiply(k)
 
-    def wait_query(t, carry):
-        other = (inner + t) % inners
-        spread_copy(other, other).wait()
-        return carry
-
-    lax.fori_loop(1, inners, wait_query, 0)
+    for copy in spread_copies:
+        copy.wait()
+    twin_copy = remote(
+        query_parts.at[core], query_parts.at[core], spread_send.at[3], spread_recv.at[3],
+        outer, twin,
+    )
+    twin_copy.start()
+    relay(2)
+    relay(3)
+    twin_copy.wait()
     for pair in range(4):
         query[pair * 16 : (pair + 1) * 16] = jnp.concatenate(
-            [query_parts[pair * 2], query_parts[pair * 2 + 1]], axis=0
+            [query_parts[0, pair], query_parts[1, pair]], axis=0
         ).astype(jnp.bfloat16)
     settle(0)
     settle(1)
@@ -303,8 +305,8 @@
 
     lax.fori_loop(1, devices, send_partial, 0)
 
-    relay(2)
-    relay(3)
+    relay(4)
+    relay(5)
 
     def column_copy(o):
         return remote(
@@ -339,9 +341,6 @@
     received[me] = partials[me]
     received[devices] = own_partials[me]
 
-    relay(4)
-    relay(5)
-
     def wait_partial(t, carry):
         other = (me + t) % devices
         partial_copy(other)(other).wait()
@@ -383,9 +382,6 @@
     lax.fori_loop(1, devices, send_merged, 0)
     merged_all[me] = merged[...]
 
-    for k in range(2, 6):
-        settle(k)
-
     def wait_plane(t, carry):
         other = (inner + t) % inners
         plane_copy(other, inner).wait_send()
@@ -399,6 +395,7 @@
     limit = jnp.where(column < 128, jnp.where(me > 0, anchor_length, 0), own_length)
     allowed = (place < limit) & ((column < 128) | (row >= place))
     for h in range(4):
+        settle(2 + h)
         keys = jnp.concatenate([anchor[h], context[:, h * 128 : (h + 1) * 128]], axis=0)
         values = jnp.concatenate(
             [anchor[4 + h], context[:, 512 + h * 128 : 512 + (h + 1) * 128]], axis=0
@@ -438,7 +435,7 @@
         ((4, 128, 1024), bf16), ((4, 64, 1024), bf16), ((4, 128, 1024), bf16),
         ((4, 6, 128, 512), f32), ((6, 128, 512), f32), ((6, 128, 512), f32),
         ((6, 128, 512), f32), ((64, 3072), f32), ((3, 8, 3072), f32), ((8, 3072), f32),
-        ((8, 8, 3072), f32), ((128, 3072), bf16), ((64, 3072), bf16),
+        ((2, 4, 8, 3072), f32), ((128, 3072), bf16), ((64, 3072), bf16),
         ((8, 128, 128), bf16), ((32, 40, 128), f32), ((32, 40, 128), f32),
         ((33, 40, 128), f32), ((32, 128), bf16), ((32, 32, 128), bf16),
     ]
@@ -454,7 +451,7 @@
         scratch_shapes=[pltpu.VMEM(shape, kind) for shape, kind in buffers]
         + [dma((count,)) for count in counts],
         compiler_params=pltpu.CompilerParams(
-            collective_id=0, has_side_effects=True, vmem_limit_bytes=56 * 2**20
+            collective_id=0, has_side_effects=True, vmem_limit_bytes=40 * 2**20
         ),
         cost_estimate=pl.CostEstimate(
             flops=5 * 10**9, bytes_accessed=8 * 2**20, transcendentals=10**6

time: 109 us -> 112 us (1.028)
  local copies, waits for them, and re-layouts: 3.55 us -> 8.8 us
  Pallas kernels: 104 us -> 102 us
    unnamed x2 -> x16, local copies, waits for them, and re-layouts: 3.55 us -> 8.8 us
    pallas_call x1, Pallas kernels: 104 us -> 102 us  [layer(): pl.pallas_call(layer_kernel, out_shape=[jax.ShapeDtypeStruct((128, 2048),...]
where the time goes in v1:
time: 112 us; the launch traced here: 111 us
  Pallas kernels  102 us (91%)
  local copies, waits for them, and re-layouts  8.8 us (8%)
    pallas_call x1, Pallas kernels, layer(): pl.pallas_call(layer_kernel, out_shape=[jax.ShapeDtypeStruct((128, 2048),...  102 us
    unnamed x16, local copies, waits for them, and re-layouts  8.8 us

profile of v1, /device:TPU:9, one launch (start us, length us, event | category | flops | bytes accessed | tf_op | source)
XLA Modules:
  0.0 111.2 jit_solution(13433775132755635221)
XLA Ops:
  0.6 0.0 copy-start
  0.6 1.6 %copy-done = bf16[512,2048]{1,0:T(8,128)(2,1)S(1)} copy-done((bf16[512,2048]{1,0:T(8,128)(2,1)S(1)}, bf16[512,2048]{1,0:T(8,128)(2,1)}, u32[]{:S(2)}) %copy-start) | copy-done | bytes 2097176
  2.2 0.0 copy-start.1
  2.2 1.2 %copy-done.1 = bf16[128,4096]{1,0:T(8,128)(2,1)S(1)} copy-done((bf16[128,4096]{1,0:T(8,128)(2,1)S(1)}, bf16[128,4096]{1,0:T(8,128)(2,1)}, u32[]{:S(2)}) %copy-start.1) | copy-done | bytes 1048600
  3.4 0.0 copy-start.2
  3.5 1.0 copy-done.2
  4.5 0.0 copy-start.3
  4.5 1.0 copy-done.3
  5.5 0.0 copy-start.4
  5.5 1.0 copy-done.4
  6.6 0.0 copy-start.5
  6.6 0.7 copy-done.5
  7.3 0.0 copy-start.6
  7.3 0.7 copy-done.6
  7.9 101.8 %shard_map.86 = (bf16[128,2048]{1,0:T(8,128)(2,1)S(1)}, bf16[64,2048]{1,0:T(8,128)(2,1)S(1)}) custom-call(bf16[128,4096]{1,0:T(8,128)(2,1)S(1)} %copy-done.1, bf16[64,4096]{1,0:T(8,128)(2,1)S(1)} %copy-done.2, f32[1,4096]{1,0:T(1,128)S(1)} %bitcast.1, bf16[512,2048]{1,0:T(8,128)(2,1)S(1)} %copy-done, bf16[512,512]{1,0:T(8,128)(2,1)S(1)} %copy-done.3, ...), custom_call_target="tpu_custom_call" | custom-call | flops 5000000000 | bytes 8388608 | tf_op jit(solution)/shard_map/pallas_call | solution.py:443
  109.7 0.8 copy.11
  110.5 0.7 copy.12
Async XLA Ops:
  0.6 1.6 %copy-start = (bf16[512,2048]{1,0:T(8,128)(2,1)S(1)}, bf16[512,2048]{1,0:T(8,128)(2,1)}, u32[]{:S(2)}) copy-start(bf16[512,2048]{1,0:T(8,128)(2,1)} %w_query.1) | copy-start | bytes 6291460
  2.2 1.2 %copy-start.1 = (bf16[128,4096]{1,0:T(8,128)(2,1)S(1)}, bf16[128,4096]{1,0:T(8,128)(2,1)}, u32[]{:S(2)}) copy-start(bf16[128,4096]{1,0:T(8,128)(2,1)} %context_rows.1) | copy-start | bytes 3145732
  3.4 1.0 copy-start.2
  4.5 1.0 copy-start.3
  5.5 1.0 copy-start.4
  6.6 0.7 copy-start.5
  7.3 0.7 copy-start.6
